TPU v7x, 32 devices: a whole 2x2x4 slice. The times are simulated.
32 devices in a mesh: sample: 2 (over y), gx: 8 (over z, x), gy: 2 (over core).
Axes of the slice: x: 2, y: 2, z: 4, core: 2. Of those that a mesh axis runs over, the one named last changes fastest.
Arguments:
- displacement: float32 [2, 128, 1024], P(None, ('sample', 'gx'), 'gy'), parts along dimension 1, may hold values from -5 to 5
- velocity: float32 [2, 128, 1024], P(None, ('sample', 'gx'), 'gy'), parts along dimension 1, may hold values from -5 to 5
- pressure: float32 [128, 1024], P(('sample', 'gx'), 'gy'), parts along dimension 0, may hold values from -5 to 5
- broken_bits: int32 [10, 128, 1024], P(None, ('sample', 'gx'), 'gy'), parts along dimension 1, may hold values from 0 to 4095
- material_class: int32 [128, 1024], P(('sample', 'gx'), 'gy'), parts along dimension 0, may hold values from 0 to 3
- property_table: float32 [8, 4], P('sample'), parts along dimension 0, may hold values from 0.5 to 2
Outputs:
- final_displacement: float32 [2, 128, 1024], P(None, ('sample', 'gx'), 'gy'), parts along dimension 1
- final_velocity: float32 [2, 128, 1024], P(None, ('sample', 'gx'), 'gy'), parts along dimension 1
- final_pressure: float32 [128, 1024], P(('sample', 'gx'), 'gy'), parts along dimension 0
There are 2 independent parts, one for each index of `sample`. A program takes and returns all parts, laid end to end along the dimension named above; each array names one. Nothing has to cross between parts.
Inputs may be any that keep to these rules, and one draw needn't show every extreme that they name: `broken_bits`: bits 12 and above of each word are 0.
All inputs are finite; a program needn't handle non-finite values.
Results may differ from a plain program's by a relative error of at most 0.00002.
Values sent between devices are 32-bit elements; how exact they have to be, the bound alone decides.
A program may use at most 64 MiB of HBM per device.

v0:
```python
import functools
import math

import jax
import jax.numpy as jnp
from jax import lax
from jax.experimental import pallas as pl
from jax.experimental.pallas import tpu as pltpu
from jax.sharding import PartitionSpec as P

REACH = 6
MESH = pl.DeviceIdType.MESH
LANES = 128
FAR = 3.0e38

half_width = {a: math.isqrt(37 - a * a) for a in range(-REACH, REACH + 1)}
first_bond = {}
_count = 0
for _a in range(-REACH, REACH + 1):
    first_bond[_a] = _count
    _count += 2 * half_width[_a] + 1 - (1 if _a == 0 else 0)
BONDS = _count

groups = (
    ((-1, 0, 1), (-6, -5, -4, -3, -2, -1, 1, 2, 3, 4, 5, 6)),
    ((-3, -2, 2, 3), tuple(range(-5, 6))),
    ((-4, 4), tuple(range(-4, 5))),
    ((-5, 5), tuple(range(-3, 4))),
    ((-6, 6), tuple(range(-1, 2))),
    ((-1, 1), (0,)),
)


def pick(index, values):
    if isinstance(index, int) or len(set(values)) == 1:
        return values[index if isinstance(index, int) else 0]
    kind = jnp.int32 if isinstance(values[0], int) else jnp.float32
    result = kind(values[-1])
    for i in range(len(values) - 2, -1, -1):
        result = jnp.where(index <= i, kind(values[i]), result)
    return result


def f32(values):
    return [float(v) for v in values]


def over_bonds(carry, visit):
    for cols, rows in groups:

        def body(i, carry, cols=cols, rows=rows):
            b = pick(i, list(cols))
            for a in rows:
                k = first_bond[a] + b + half_width[a]
                if a == 0:
                    k = k - pick(i, [1 if c > 0 else 0 for c in cols])
                carry = visit(carry, i, a, cols, b + REACH, k)
            return carry

        for i in range(len(cols)):
            carry = body(i, carry)
    return carry


def kernel(
    gx_count, disp, vel, pres, bits, klass, table,
    out_disp, out_vel, out_pres,
    x1, x2, kl, inv, shifted, shifted_inv, wc, wk, bits_v, vel_v,
    local_sem, send_sem, recv_sem, send2_sem, recv2_sem,
):
    sample, gx, gy = lax.axis_index("sample"), lax.axis_index("gx"), lax.axis_index("gy")
    height, breadth = pres.shape
    wide = breadth + LANES
    own = pl.ds(height, height)
    up_rows, down_rows = pl.ds(0, height), pl.ds(2 * height, height)
    cols, side = pl.ds(0, breadth), pl.ds(breadth, LANES)
    edge = pl.ds(pl.multiple_of((1 - gy) * (breadth - LANES), LANES), LANES)
    has_up, has_down = gx > 0, gx < gx_count - 1
    up, down, mate = gx - 1, gx + 1, 1 - gy

    local = [
        pltpu.make_async_copy(klass, kl.at[own, cols], local_sem.at[0]),
        pltpu.make_async_copy(disp, x1.at[pl.ds(0, 2), own, cols], local_sem.at[1]),
        pltpu.make_async_copy(pres, x1.at[2, own, cols], local_sem.at[2]),
        pltpu.make_async_copy(bits, bits_v, local_sem.at[3]),
        pltpu.make_async_copy(vel, vel_v, local_sem.at[4]),
    ]
    for copy in local:
        copy.start()

    barrier = pltpu.get_barrier_semaphore()

    def greet(x, y):
        pl.semaphore_signal(barrier, inc=1, device_id=(sample, x, y), device_id_type=MESH)

    greet(gx, mate)

    @pl.when(has_up)
    def _():
        greet(up, gy)
        greet(up, mate)

    @pl.when(has_down)
    def _():
        greet(down, gy)
        greet(down, mate)

    @pl.when(jnp.logical_not(has_up))
    def _():
        for ref in (x1, x2):
            ref[:, 0:height, :] = jnp.zeros((3, height, wide), jnp.float32)
        kl[0:height, :] = jnp.zeros((height, wide), jnp.int32)

    @pl.when(jnp.logical_not(has_down))
    def _():
        for ref in (x1, x2):
            ref[:, 2 * height : 3 * height, :] = jnp.zeros((3, height, wide), jnp.float32)
        kl[2 * height : 3 * height, :] = jnp.zeros((height, wide), jnp.int32)

    pl.semaphore_wait(
        barrier, 1 + 2 * has_up.astype(jnp.int32) + 2 * has_down.astype(jnp.int32)
    )

    routes = (
        (has_up, has_down, (sample, up, gy), down_rows, True),
        (has_down, has_up, (sample, down, gy), up_rows, True),
        (None, None, (sample, gx, mate), own, False),
        (has_up, has_down, (sample, up, mate), down_rows, False),
        (has_down, has_up, (sample, down, mate), up_rows, False),
    )

    def when(condition, act):
        if condition is None:
            act()
        else:
            pl.when(condition)(act)

    def remote(n, source, target, sends, recvs):
        return pltpu.make_async_remote_copy(
            src_ref=source, dst_ref=target, send_sem=sends.at[n], recv_sem=recvs.at[n],
            device_id=routes[n % 5][2], device_id_type=MESH,
        )

    first = []
    for which in range(2):
        for n, (_, _, _, there, whole) in enumerate(routes):
            here, land = (cols, cols) if whole else (edge, side)
            if which == 0:
                source, target = klass.at[:, here], kl.at[there, land]
            else:
                source, target = x1.at[:, own, here], x1.at[:, there, land]
            first.append(remote(which * 5 + n, source, target, send_sem, recv_sem))
    for i, copy in enumerate(first):
        if i == 5:
            local[1].wait()
            local[2].wait()
        when(routes[i % 5][0], copy.start)

    for i in range(5):
        when(routes[i][1], first[i].wait_recv)
    local[0].wait()
    local[3].wait()

    row = lax.broadcasted_iota(jnp.int32, (3 * height, wide), 0)
    col = lax.broadcasted_iota(jnp.int32, (3 * height, wide), 1)
    low, high = jnp.where(has_up, 0, height), jnp.where(has_down, 3 * height, 2 * height)
    middle = breadth + LANES // 2
    left_side = jnp.where(gy == 0, breadth, middle)
    right_side = jnp.where(gy == 0, middle, wide)
    inside = (row >= low) & (row < high) & (
        (col < breadth) | ((col >= left_side) & (col < right_side))
    )
    classes = table.shape[0]

    def look_up(which, member):
        value = jnp.full(which.shape, table[classes - 1, member], jnp.float32)
        for c in range(classes - 1):
            value = jnp.where(which == c, table[c, member], value)
        return value

    which = kl[...]
    for m in range(2):
        inv[m] = jnp.where(inside, 1.0 / look_up(which, m), FAR)

    def shift_all(source, planes, target):
        for plane in range(planes):
            for t in range(3):
                rows = pl.ds(t * height, height)
                value = source[plane, rows, :]
                for b in range(-REACH, REACH + 1):
                    moved = value if b == 0 else pltpu.roll(value, (-b) % wide, 1)
                    target[b + REACH, plane, rows, :] = moved[:, :breadth]

    shift_all(inv, 2, shifted_inv)
    ic, ik = inv[0, height : 2 * height, :breadth], inv[1, height : 2 * height, :breadth]

    def weigh(carry, i, a, steps, shift, k):
        rows = pl.ds(height + a, height)
        intact = (bits_v[k // 12] & lax.shift_left(jnp.int32(1), k % 12)) == 0
        for here, plane, target in ((ic, 0, wc), (ik, 1, wk)):
            total = here + shifted_inv[shift, plane, rows, :]
            guess = pl.reciprocal(total, approx=True)
            exact = guess * (2.0 - total * guess)
            target[k] = jnp.where(intact, exact, 0.0)
        return carry

    over_bonds(0, weigh)

    for i in range(5, 10):
        when(routes[i % 5][1], first[i].wait_recv)
    local[4].wait()

    own_class = kl[height : 2 * height, :breadth]
    density = look_up(own_class, 2)
    storage = look_up(own_class, 3)

    def advance(x, velocity):
        u0, u1, p = (x[f, height : 2 * height, :breadth] for f in range(3))
        shift_all(x, 3, shifted)

        def visit(carry, i, a, steps, shift, k):
            force_x, force_y, dilation, inflow = carry
            rows = pl.ds(height + a, height)
            squares = [a * a + b * b for b in steps]
            q = shifted[shift, 2, rows, :]
            scaled_y = pick(i, f32(2.0 * b / s**2 for b, s in zip(steps, squares)))
            part = scaled_y * (shifted[shift, 1, rows, :] - u1)
            if a != 0:
                scaled_x = pick(i, f32(2.0 * a / s**2 for s in squares))
                part = part + scaled_x * (shifted[shift, 0, rows, :] - u0)
            weight = wc[k]
            pull = weight * part
            mag = pull - weight * (pick(i, f32(0.5 / s for s in squares)) * (q + p))
            if a != 0:
                force_x = force_x + float(a) * mag
            force_y = force_y + pick(i, f32(steps)) * mag
            dilation = dilation + pick(i, f32(math.sqrt(s) for s in squares)) * pull
            inflow = inflow + wk[k] * (pick(i, f32(2.0 / s for s in squares)) * (q - p))
            return force_x, force_y, dilation, inflow

        zero = jnp.zeros((height, breadth), jnp.float32)
        force_x, force_y, dilation, inflow = over_bonds((zero,) * 4, visit)
        v0 = velocity[0] + 0.1 * (density * force_x - 0.5 * velocity[0])
        v1 = velocity[1] + 0.1 * (density * force_y - 0.5 * velocity[1])
        return (
            u0 + 0.1 * v0, u1 + 0.1 * v1, p + 0.1 * storage * 0.1 * (inflow - dilation), v0, v1
        )

    n0, n1, np_, v0, v1 = advance(x1, (vel_v[0], vel_v[1]))
    x2[0, height : 2 * height, :breadth] = n0
    x2[1, height : 2 * height, :breadth] = n1
    x2[2, height : 2 * height, :breadth] = np_
    vel_v[0] = v0
    vel_v[1] = v1

    second = []
    for n, (_, _, _, there, whole) in enumerate(routes):
        here, land = (cols, cols) if whole else (edge, side)
        second.append(
            remote(n, x2.at[:, own, here], x2.at[:, there, land], send2_sem, recv2_sem)
        )
    for i, copy in enumerate(second):
        when(routes[i][0], copy.start)
    for i, copy in enumerate(second):
        when(routes[i][1], copy.wait_recv)

    n0, n1, np_, v0, v1 = advance(x2, (vel_v[0], vel_v[1]))
    out_disp[0] = n0
    out_disp[1] = n1
    out_vel[0] = v0
    out_vel[1] = v1
    out_pres[...] = np_

    for i, copy in enumerate(first):
        when(routes[i % 5][0], copy.wait_send)
    for i, copy in enumerate(second):
        when(routes[i][0], copy.wait_send)


def body(gx_count, displacement, velocity, pressure, broken_bits, material_class, table):
    height, breadth = pressure.shape
    wide = breadth + LANES
    vmem = pl.BlockSpec(memory_space=pltpu.VMEM)
    anywhere = pl.BlockSpec(memory_space=pltpu.HBM)
    smem = pl.BlockSpec(memory_space=pltpu.SMEM)
    f = jnp.float32
    dma = pltpu.SemaphoreType.DMA
    span = 2 * REACH + 1
    return pl.pallas_call(
        functools.partial(kernel, gx_count),
        out_shape=(
            pltpu.VMEM((2, height, breadth), f),
            pltpu.VMEM((2, height, breadth), f),
            pltpu.VMEM((height, breadth), f),
        ),
        in_specs=[anywhere] * 5 + [smem],
        out_specs=(vmem, vmem, vmem),
        scratch_shapes=[
            pltpu.VMEM((3, 3 * height, wide), f),
            pltpu.VMEM((3, 3 * height, wide), f),
            pltpu.VMEM((3 * height, wide), jnp.int32),
            pltpu.VMEM((2, 3 * height, wide), f),
            pltpu.VMEM((span, 3, 3 * height, breadth), f),
            pltpu.VMEM((span, 2, 3 * height, breadth), f),
            pltpu.VMEM((BONDS, height, breadth), f),
            pltpu.VMEM((BONDS, height, breadth), f),
            pltpu.VMEM(broken_bits.shape, jnp.int32),
            pltpu.VMEM((2, height, breadth), f),
            dma((5,)), dma((10,)), dma((10,)), dma((5,)), dma((5,)),
        ],
        compiler_params=pltpu.CompilerParams(
            collective_id=0, has_side_effects=True, vmem_limit_bytes=62 * 1024 * 1024
        ),
        name="peridynamics",
    )(displacement, velocity, pressure, broken_bits, material_class, table)


def solution(mesh):
    plane = P(("sample", "gx"), "gy")
    stack = P(None, ("sample", "gx"), "gy")
    assert mesh.shape["gy"] == 2
    return jax.shard_map(
        functools.partial(body, mesh.shape["gx"]),
        mesh=mesh,
        in_specs=(stack, stack, plane, stack, plane, P("sample", None)),
        out_specs=(stack, stack, plane),
        check_vma=False,
    )
```

profile of v0, /device:TPU:11, one launch (start us, length us, event | category | flops | bytes accessed | tf_op | source)
XLA Modules:
  0.0 21.6 jit_solution(10311594571702814780)
XLA Ops:
  0.6 19.1 %peridynamics.1 = (f32[2,8,512]{2,1,0:T(8,128)S(1)}, f32[2,8,512]{2,1,0:T(8,128)S(1)}, f32[8,512]{1,0:T(8,128)S(1)}) custom-call(f32[2,8,512]{2,1,0:T(8,128)} %disp.1, f32[2,8,512]{2,1,0:T(8,128)} %vel.1, f32[8,512]{1,0:T(8,128)} %pres.1, s32[10,8,512]{2,1,0:T(8,128)} %bits.1, s32[8,512]{1,0:T(8,128)} %klass.1, f32[4,4]{1,0:T(4,128)} %table.1), custom_call_target="tpu_custom_call" | custom-call | tf_op jit(solution)/shard_map/peridynamics/pallas_call | solution.py:289
  19.7 0.6 %copy.12 = f32[2,8,512]{2,1,0:T(8,128)} copy(f32[2,8,512]{2,1,0:T(8,128)S(1)} %get-tuple-element.3) | data formatting | bytes 65536
  20.4 0.6 %copy.14 = f32[8,512]{1,0:T(8,128)} copy(f32[8,512]{1,0:T(8,128)S(1)} %get-tuple-element.5) | data formatting | bytes 32768
  21.0 0.6 %copy.13 = f32[2,8,512]{2,1,0:T(8,128)} copy(f32[2,8,512]{2,1,0:T(8,128)S(1)} %get-tuple-element.4) | data formatting | bytes 65536
where the time goes:
time: 21.8 us; the launch traced here: 21.6 us
  Pallas kernels  19.1 us (88%)
  local copies, waits for them, and re-layouts  1.84 us (8%)
  between operations  0.64 us (3%)
    pallas_call x1, Pallas kernels, body(): pl.pallas_call(functools.partial(kernel, gx_count), out_shape=(pltpu.VMEM...  19.1 us
    unnamed x3, local copies, waits for them, and re-layouts  1.84 us

commit v1 on v0

v1 whole, which is shorter than its diff:
```python
import functools
import math

import jax
import jax.numpy as jnp
from jax import lax
from jax.experimental import pallas as pl
from jax.experimental.pallas import tpu as pltpu
from jax.sharding import PartitionSpec as P

REACH = 6
SPAN = 2 * REACH + 1
MESH = pl.DeviceIdType.MESH
LANES = 128
ROWS = 8
OUTSIDE = -1
FAR = 3.0e38

half_width = {a: math.isqrt(37 - a * a) for a in range(-REACH, REACH + 1)}
first_bond = {}
_count = 0
for _a in range(-REACH, REACH + 1):
    first_bond[_a] = _count
    _count += 2 * half_width[_a] + 1 - (1 if _a == 0 else 0)


def bond(a, b):
    if abs(a) > REACH or abs(b) > half_width[a] or (a == 0 and b == 0):
        return None
    return first_bond[a] + b + half_width[a] - (1 if a == 0 and b > 0 else 0)


def groups_of(own):
    out = [(0, 0, 0)] if own else []
    for o in range(1, ROWS):
        out.append((o, o, o - ROWS) if own else (o, o - ROWS, o))
    return out


def columns_of(low, high):
    return max(half_width.get(low, -1), half_width.get(high, -1))


def slots_of(own):
    slots = {}
    for o, low, high in groups_of(own):
        for b in range(-columns_of(low, high), columns_of(low, high) + 1):
            if (o, b) != (0, 0):
                slots[o, b] = len(slots)
    return slots


SLOTS = {own: slots_of(own) for own in (True, False)}


def kernel(
    gx_count, disp, vel, pres, bits, klass, table,
    out_disp, out_vel, out_pres,
    disp_v, vel_v, pres_v, bits_v, klass_v, table_s,
    own1, far1, own2, far2,
    z_own, z_far, q_own, q_far, inv_own, inv_far, inverse, here_inv,
    w_own, v_own, w_far, v_far, ex_far, side_b, still,
    local_sem, send_sem, recv_sem, send2_sem, recv2_sem,
):
    f32 = jnp.float32
    sample, gx, gy = lax.axis_index("sample"), lax.axis_index("gx"), lax.axis_index("gy")
    height, breadth = pres.shape
    blocks = breadth // LANES
    has_up, has_down = gx > 0, gx < gx_count - 1
    up, down, mate = gx - 1, gx + 1, 1 - gy

    local = [
        pltpu.make_async_copy(table, table_s, local_sem.at[0]),
        pltpu.make_async_copy(klass, klass_v, local_sem.at[1]),
        pltpu.make_async_copy(disp, disp_v, local_sem.at[2]),
        pltpu.make_async_copy(pres, pres_v, local_sem.at[3]),
        pltpu.make_async_copy(bits, bits_v, local_sem.at[4]),
        pltpu.make_async_copy(vel, vel_v, local_sem.at[5]),
    ]
    for copy in local:
        copy.start()

    for plane in range(4):
        fill = float(OUTSIDE) if plane == 3 else 0.0
        far1[plane] = jnp.full(far1.shape[1:], fill, f32)
        if plane < 3:
            far2[plane] = jnp.zeros(far2.shape[1:], f32)

    barrier = pltpu.get_barrier_semaphore()

    def greet(x, y):
        pl.semaphore_signal(barrier, inc=1, device_id=(sample, x, y), device_id_type=MESH)

    @pl.when(has_up)
    def _():
        greet(up, gy)
        greet(up, mate)

    @pl.when(has_down)
    def _():
        greet(down, gy)
        greet(down, mate)

    greet(gx, mate)

    def cut(value):
        return [value[:, j * LANES : (j + 1) * LANES] for j in range(blocks)]

    def put(target, plane, value):
        for j, piece in enumerate(cut(value)):
            for rows in (slice(0, ROWS), slice(ROWS, 2 * ROWS)):
                target[plane, j, rows, :] = piece

    for i in (1, 2, 3):
        local[i].wait()
    put(own1, 3, klass_v[...].astype(f32))
    put(own1, 0, disp_v[0])
    put(own1, 1, disp_v[1])
    put(own1, 2, pres_v[...])

    sides = pl.ds(0, blocks)
    edge, rim = pl.ds((1 - gy) * (blocks - 1), 1), pl.ds(blocks, 1)
    to_up = (pl.ds(0, REACH), pl.ds(ROWS, REACH))
    to_down = (pl.ds(ROWS - REACH, REACH), pl.ds(ROWS - REACH, REACH))
    routes = (
        (has_up, has_down, (sample, up, gy), to_up, True),
        (has_down, has_up, (sample, down, gy), to_down, True),
        (has_up, has_down, (sample, up, mate), to_up, False),
        (has_down, has_up, (sample, down, mate), to_down, False),
        (None, None, (sample, gx, mate), None, False),
    )

    def when(condition, act):
        if condition is None:
            act()
        else:
            pl.when(condition)(act)

    def exchange(own, far, sends, recvs):
        copies = []
        for n, (_, _, device, rows, whole) in enumerate(routes):
            here, land = (sides, sides) if whole else (edge, rim)
            if rows is None:
                source, target = own.at[:, here, pl.ds(0, ROWS)], own.at[:, land, pl.ds(0, ROWS)]
            else:
                source, target = own.at[:, here, rows[0]], far.at[:, land, rows[1]]
            copies.append(
                pltpu.make_async_remote_copy(
                    src_ref=source, dst_ref=target, send_sem=sends.at[n], recv_sem=recvs.at[n],
                    device_id=device, device_id_type=MESH,
                )
            )
        return copies

    def start(copies):
        for n, copy in enumerate(copies):
            when(routes[n][0], copy.start)

    def arrive(copies, which):
        for n in which:
            when(routes[n][1], copies[n].wait_recv)

    pl.semaphore_wait(
        barrier, 1 + 2 * has_up.astype(jnp.int32) + 2 * has_down.astype(jnp.int32)
    )
    first = exchange(own1, far1, send_sem, recv_sem)
    start(first)

    sublane = lax.broadcasted_iota(jnp.int32, (ROWS, LANES), 0)
    lane = lax.broadcasted_iota(jnp.int32, (ROWS, LANES), 1)

    def mix(o, low, high, kind=f32):
        return kind(low) if low == high else jnp.where(sublane < ROWS - o, kind(low), kind(high))

    local[0].wait()

    def look_up(which, member):
        value = jnp.full(which.shape, table_s[table.shape[0] - 1, member], f32)
        for c in range(table.shape[0] - 1):
            value = jnp.where(which == c, table_s[c, member], value)
        return value

    classes = table.shape[0]
    for m in range(2):
        for c in range(classes):
            inverse[m, c] = 1.0 / jnp.full((ROWS, LANES), table_s[c, m], f32)

    def inverses(which):
        out = [jnp.full(which.shape, FAR, f32)] * 2
        for c in range(classes):
            chosen = which == float(c)
            out = [jnp.where(chosen, inverse[m, c], out[m]) for m in range(2)]
        return out

    for m, value in enumerate(inverses(own1[3, :blocks, 0:ROWS, :])):
        here_inv[m] = value

    klass_own = klass_v[...]
    for plane, member in ((0, 2), (1, 3)):
        for j, piece in enumerate(cut(look_up(klass_own, member))):
            still[plane, j] = piece
    local[4].wait()
    for j in range(blocks):
        words = [bits_v[w, :, j * LANES : (j + 1) * LANES] for w in range(bits.shape[0])]

        def broken(a, b):
            k = bond(a, b)
            return jnp.int32(1) if k is None else words[k // 12] & (1 << (k % 12))

        for own, w_to, v_to in ((True, w_own, v_own), (False, w_far, v_far)):
            for o, low, high in groups_of(own):
                for b in range(-columns_of(low, high), columns_of(low, high) + 1):
                    if (o, b) not in SLOTS[own]:
                        continue
                    n = SLOTS[own][o, b]
                    one = broken(low, b)
                    if o:
                        one = jnp.where(sublane < ROWS - o, one, broken(high, b))
                    squares = [a * a + b * b for a in (low, high)]
                    w_to[n, j] = jnp.where(one == 0, mix(o, *[2.0 / x**2 for x in squares]), 0.0)
                    v_to[n, j] = jnp.where(one == 0, mix(o, *[2.0 / x for x in squares]), 0.0)

    def shift(value, b):
        if b == 0:
            return value[:blocks]
        turned = pltpu.roll(value, (-b) % LANES, 2)
        if b > 0:
            return jnp.where(lane < LANES - b, turned[:blocks], turned[1:])
        before = jnp.concatenate([turned[blocks:], turned[: blocks - 1]], axis=0)
        return jnp.where(lane >= -b, turned[:blocks], before)

    def tiles(own):
        top, bottom = slice(0, ROWS), slice(ROWS, 2 * ROWS)
        return [(top, (top, bottom))] if own else [(top, (top,)), (bottom, (bottom,))]

    valid = (lane < LANES // 2) == (gy == 0)

    def materials(own, x, target):
        for read, write in tiles(own):
            value = x[3, :, read, :]
            rim_value = jnp.where(valid, value[blocks:], float(OUTSIDE))
            value = jnp.concatenate([value[:blocks], rim_value], axis=0)
            for m, value in enumerate(inverses(value)):
                for b in range(-REACH, REACH + 1):
                    moved = shift(value, b)
                    for rows in write:
                        target[m, b + REACH, :, rows, :] = moved

    def prepare(own, x, z, q_moved):
        for read, write in tiles(own):
            v, q = x[1, :, read, :], x[2, :, read, :]
            for b in range(-REACH, REACH + 1):
                moved = shift(q, b)
                for rows in write:
                    q_moved[b + REACH, :, rows, :] = moved
            for b in range(1, REACH + 1):
                bv, bq = float(b) * v, (-0.25 * b * b) * q
                for rows in write:
                    z[REACH + b, :, rows, :] = bq + bv
                    z[REACH - b, :, rows, :] = bq - bv

    def centre(x):
        v, p = x[1, :blocks, 0:ROWS, :], x[2, :blocks, 0:ROWS, :]
        for b in range(-REACH, REACH + 1):
            if b:
                side_b[b + REACH] = float(b) * v + (0.25 * b * b) * p

    def row_centre(x, o, low, high):
        u, p = x[0, :blocks, 0:ROWS, :], x[2, :blocks, 0:ROWS, :]
        return mix(o, low, high) * u + mix(o, 0.25 * low * low, 0.25 * high * high) * p

    def centre_far(x):
        for o, low, high in groups_of(False):
            here = row_centre(x, o, low, high)
            for b in range(-columns_of(low, high), columns_of(low, high) + 1):
                n = SLOTS[False][o, b]
                ex_far[n] = here if b == 0 else here + side_b[b + REACH]

    def evaluate(own, x, z, q_moved, sums, fresh):
        w_ref, v_ref = (w_own, v_own) if own else (w_far, v_far)
        inv = inv_own if own else inv_far
        slots = SLOTS[own]
        force_x, force_y, gain, drain = sums
        for o, low, high in groups_of(own):
            rows = pl.ds(o, ROWS)
            wide = columns_of(low, high)
            if o:
                y = (
                    mix(o, low, high) * x[0, :, rows, :]
                    - mix(o, 0.25 * low * low, 0.25 * high * high) * x[2, :, rows, :]
                )
            if own and o:
                here = row_centre(x, o, low, high)
            row_sum = None

            def one(b):
                n = slots[o, b]
                if fresh:
                    cubes = [0.25 * math.sqrt(a * a + b * b) ** 3 for a in (low, high)]
                    weight, flow = (
                        ref[n]
                        * pl.reciprocal(
                            here_inv[m] + inv[m, b + REACH, :, rows, :], approx=True
                        )
                        for m, ref in enumerate((w_ref, v_ref))
                    )
                    share = mix(o, *cubes) * weight
                    lost, flow = flow + share, flow - share
                    w_ref[n] = weight
                    v_ref[n] = flow
                else:
                    weight, flow, lost = w_ref[n], v_ref[n], None
                if b == 0:
                    there = y[:blocks]
                else:
                    there = z[b + REACH, :, rows, :]
                    there = shift(y + there if o else there, b)
                if not own:
                    mine = ex_far[n]
                elif o == 0:
                    mine = side_b[b + REACH]
                else:
                    mine = here if b == 0 else here + side_b[b + REACH]
                mag = weight * (there - mine)
                return mag, flow * q_moved[b + REACH, :, rows, :], lost

            for b in range(wide + 1):
                if (o, b) not in slots:
                    continue
                length = mix(o, *[math.sqrt(a * a + b * b) for a in (low, high)])
                mag, flow, lost = one(b)
                gain = gain + flow
                if fresh:
                    drain = drain + lost
                if b:
                    mag2, flow, lost = one(-b)
                    gain = gain + flow
                    if fresh:
                        drain = drain + lost
                    force_y = force_y + float(b) * (mag - mag2)
                    mag = mag + mag2
                gain = gain - length * mag
                row_sum = mag if row_sum is None else row_sum + mag
            if o:
                force_x = force_x + mix(o, low, high) * row_sum
        return force_x, force_y, gain, drain

    def duplicate_rim(x, planes):
        for plane in range(planes):
            x[plane, blocks, ROWS : 2 * ROWS, :] = x[plane, blocks, 0:ROWS, :]

    def half_step(x, z, q, sums, fresh):
        prepare(True, x, z, q)
        centre(x)
        centre_far(x)
        return evaluate(True, x, z, q, sums, fresh)

    def finish(x, sums, drain, velocity):
        force_x, force_y, gain, _ = sums
        u0, u1, p = (x[plane, :blocks, 0:ROWS, :] for plane in range(3))
        density, storage = still[0], still[1]
        v0 = velocity[0] + 0.1 * (density * force_x - 0.5 * velocity[0])
        v1 = velocity[1] + 0.1 * (density * force_y - 0.5 * velocity[1])
        pressure = p + 0.1 * storage * 0.1 * (gain - drain * p)
        return u0 + 0.1 * v0, u1 + 0.1 * v1, pressure, v0, v1

    zero = jnp.zeros((blocks, ROWS, LANES), f32)

    arrive(first, (4,))
    duplicate_rim(own1, 4)
    materials(True, own1, inv_own)
    sums = half_step(own1, z_own, q_own, (zero,) * 4, True)
    local[5].wait()
    velocity = [jnp.stack(cut(vel_v[i])) for i in range(2)]

    arrive(first, (0, 1, 2, 3))
    materials(False, far1, inv_far)
    prepare(False, far1, z_far, q_far)
    sums = evaluate(False, far1, z_far, q_far, sums, True)
    drain = sums[3]
    n0, n1, np_, v0, v1 = finish(own1, sums, drain, velocity)
    for plane, value in enumerate((n0, n1, np_)):
        own2[plane, :blocks, 0:ROWS, :] = value
        own2[plane, :blocks, ROWS : 2 * ROWS, :] = value

    second = exchange(own2, far2, send2_sem, recv2_sem)
    start(second)
    arrive(second, (4,))
    duplicate_rim(own2, 3)
    sums = half_step(own2, z_own, q_own, (zero,) * 4, False)
    arrive(second, (0, 1, 2, 3))
    prepare(False, far2, z_far, q_far)
    sums = evaluate(False, far2, z_far, q_far, sums, False)
    n0, n1, np_, v0, v1 = finish(own2, sums, drain, (v0, v1))

    for j in range(blocks):
        at = slice(j * LANES, (j + 1) * LANES)
        out_disp[0, :, at] = n0[j]
        out_disp[1, :, at] = n1[j]
        out_vel[0, :, at] = v0[j]
        out_vel[1, :, at] = v1[j]
        out_pres[:, at] = np_[j]

    for copies in (first, second):
        for n, copy in enumerate(copies):
            when(routes[n][0], copy.wait_send)


def hand_over(a, b, c, out_a, out_b, out_c, sems):
    copies = [
        pltpu.make_async_copy(source, target, sems.at[i])
        for i, (source, target) in enumerate(((a, out_a), (b, out_b), (c, out_c)))
    ]
    for copy in copies:
        copy.start()
    for copy in copies:
        copy.wait()


def body(gx_count, displacement, velocity, pressure, broken_bits, material_class, table):
    height, breadth = pressure.shape
    assert height == ROWS and breadth % LANES == 0 and breadth // LANES > 1
    blocks = breadth // LANES
    vmem = pl.BlockSpec(memory_space=pltpu.VMEM)
    anywhere = pl.BlockSpec(memory_space=pltpu.HBM)
    f, i32 = jnp.float32, jnp.int32
    dma = pltpu.SemaphoreType.DMA
    n_own, n_far = (len(SLOTS[own]) for own in (True, False))

    def planes(n, blocks, rows):
        return pltpu.VMEM((n, blocks, rows, LANES), f)

    shapes = (displacement.shape, velocity.shape, pressure.shape)
    results = pl.pallas_call(
        functools.partial(kernel, gx_count),
        out_shape=tuple(pltpu.VMEM(s, f) for s in shapes),
        in_specs=[anywhere] * 6,
        out_specs=(vmem, vmem, vmem),
        scratch_shapes=[
            pltpu.VMEM(displacement.shape, f),
            pltpu.VMEM(velocity.shape, f),
            pltpu.VMEM(pressure.shape, f),
            pltpu.VMEM(broken_bits.shape, i32),
            pltpu.VMEM(material_class.shape, i32),
            pltpu.SMEM(table.shape, f),
            planes(4, blocks + 1, 2 * ROWS),
            planes(4, blocks + 1, 2 * ROWS),
            planes(3, blocks + 1, 2 * ROWS),
            planes(3, blocks + 1, 2 * ROWS),
            planes(SPAN, blocks + 1, 2 * ROWS),
            planes(SPAN, blocks + 1, 2 * ROWS),
            planes(SPAN, blocks, 2 * ROWS),
            planes(SPAN, blocks, 2 * ROWS),
            pltpu.VMEM((2, SPAN, blocks, 2 * ROWS, LANES), f),
            pltpu.VMEM((2, SPAN, blocks, 2 * ROWS, LANES), f),
            planes(2, table.shape[0], ROWS),
            planes(2, blocks, ROWS),
            planes(n_own, blocks, ROWS),
            planes(n_own, blocks, ROWS),
            planes(n_far, blocks, ROWS),
            planes(n_far, blocks, ROWS),
            planes(n_far, blocks, ROWS),
            planes(SPAN, blocks, ROWS),
            planes(2, blocks, ROWS),
            dma((6,)), dma((5,)), dma((5,)), dma((5,)), dma((5,)),
        ],
        compiler_params=pltpu.CompilerParams(
            collective_id=0, has_side_effects=True, vmem_limit_bytes=62 * 1024 * 1024
        ),
        name="peridynamics",
    )(displacement, velocity, pressure, broken_bits, material_class, table)
    return pl.pallas_call(
        hand_over,
        out_shape=tuple(jax.ShapeDtypeStruct(s, f) for s in shapes),
        in_specs=[vmem] * 3,
        out_specs=(anywhere,) * 3,
        scratch_shapes=[dma((3,))],
        name="hand_over",
    )(*[pltpu.with_memory_space_constraint(r, pltpu.VMEM) for r in results])


def solution(mesh):
    plane = P(("sample", "gx"), "gy")
    stack = P(None, ("sample", "gx"), "gy")
    assert mesh.shape["gy"] == 2
    return jax.shard_map(
        functools.partial(body, mesh.shape["gx"]),
        mesh=mesh,
        in_specs=(stack, stack, plane, stack, plane, P("sample", None)),
        out_specs=(stack, stack, plane),
        check_vma=False,
    )
```

time: 21.8 us -> 14.1 us (0.65)
  the two profiles are of different devices: /device:TPU:11 before, /device:TPU:0 now
where the time goes in v1:
time: 14.1 us; the launch traced here: 14 us
  Pallas kernels  13.3 us (94%)
  between operations  0.64 us (5%)
    pallas_call x1, Pallas kernels, body(): pl.pallas_call(functools.partial(kernel, gx_count), out_shape=tuple((pltp...  12.7 us
    pallas_call x1, Pallas kernels, body(): pl.pallas_call(hand_over, out_shape=tuple((jax.ShapeDtypeStruct(s, f) for...  0.66 us

profile of v1, /device:TPU:0, one launch (start us, length us, event | category | flops | bytes accessed | tf_op | source)
XLA Modules:
  0.0 14.0 jit_solution(7098053647508486482)
XLA Ops:
  0.6 12.7 %peridynamics.1 = (f32[2,8,512]{2,1,0:T(8,128)S(1)}, f32[2,8,512]{2,1,0:T(8,128)S(1)}, f32[8,512]{1,0:T(8,128)S(1)}) custom-call(f32[2,8,512]{2,1,0:T(8,128)} %disp.1, f32[2,8,512]{2,1,0:T(8,128)} %vel.1, f32[8,512]{1,0:T(8,128)} %pres.1, s32[10,8,512]{2,1,0:T(8,128)} %bits.1, s32[8,512]{1,0:T(8,128)} %klass.1, f32[4,4]{1,0:T(4,128)} %table.1), custom_call_target="tpu_custom_call" | custom-call | tf_op jit(solution)/shard_map/peridynamics/pallas_call | solution.py:434
  13.3 0.7 %hand_over.1 = (f32[2,8,512]{2,1,0:T(8,128)}, f32[2,8,512]{2,1,0:T(8,128)}, f32[8,512]{1,0:T(8,128)}) custom-call(f32[2,8,512]{2,1,0:T(8,128)S(1)} %get-tuple-element.6.a, f32[2,8,512]{2,1,0:T(8,128)S(1)} %get-tuple-element.7.b, f32[8,512]{1,0:T(8,128)S(1)} %get-tuple-element.8.c), custom_call_target="tpu_custom_call" | custom-call | tf_op jit(solution)/shard_map/hand_over/pallas_call | solution.py:472

commit v2 on v1

v2 whole, which is shorter than its diff:
```python
import functools
import math

import jax
import jax.numpy as jnp
from jax import lax
from jax.experimental import pallas as pl
from jax.experimental.pallas import tpu as pltpu
from jax.sharding import PartitionSpec as P

REACH = 6
SPAN = 2 * REACH + 1
MESH = pl.DeviceIdType.MESH
LANES = 128
ROWS = 8
OUTSIDE = -1
PLACES = (0, 3, 1, 2)
RIM = len(PLACES)
AFTER, BEFORE = (2, RIM, 3, 1), (RIM, 3, 0, 2)
OUTER, INNER, ALL = (0, 1), (2, 3), (0, 1, 2, 3)
MESSAGES = 17
HALF = 4
FAR = 3.0e38

half_width = {a: math.isqrt(37 - a * a) for a in range(-REACH, REACH + 1)}
first_bond = {}
_count = 0
for _a in range(-REACH, REACH + 1):
    first_bond[_a] = _count
    _count += 2 * half_width[_a] + 1 - (1 if _a == 0 else 0)


def bond(a, b):
    if abs(a) > REACH or abs(b) > half_width[a] or (a == 0 and b == 0):
        return None
    return first_bond[a] + b + half_width[a] - (1 if a == 0 and b > 0 else 0)


def groups_of(own):
    out = [(0, 0, 0)] if own else []
    for o in range(1, ROWS):
        out.append((o, o, o - ROWS) if own else (o, o - ROWS, o))
    return out


def columns_of(low, high):
    return max(half_width.get(low, -1), half_width.get(high, -1))


def slots_of(own):
    slots = {}
    for o, low, high in groups_of(own):
        for b in range(-columns_of(low, high), columns_of(low, high) + 1):
            if (o, b) != (0, 0):
                slots[o, b] = len(slots)
    return slots


SLOTS = {own: slots_of(own) for own in (True, False)}


def kernel(
    gx_count, disp, vel, pres, bits, klass, table,
    out_disp, out_vel, out_pres,
    disp_v, vel_v, pres_v, bits_v, klass_v, table_s,
    own1, far1, own2, far2,
    z_own, z_far, q_own, q_far, inv_own, inv_far, inverse, here_inv,
    w_own, v_own, w_far, v_far, ex_own, ex_far, y_own, y_far, side_b, still,
    local_sem, send_sem, recv_sem,
):
    f32 = jnp.float32
    sample, gx, gy = lax.axis_index("sample"), lax.axis_index("gx"), lax.axis_index("gy")
    height, breadth = pres.shape
    blocks = breadth // LANES
    has_up, has_down = gx > 0, gx < gx_count - 1
    up, down, mate = gx - 1, gx + 1, 1 - gy

    local = [
        pltpu.make_async_copy(table, table_s, local_sem.at[0]),
        pltpu.make_async_copy(klass, klass_v, local_sem.at[1]),
        pltpu.make_async_copy(disp, disp_v, local_sem.at[2]),
        pltpu.make_async_copy(pres, pres_v, local_sem.at[3]),
        pltpu.make_async_copy(bits, bits_v, local_sem.at[4]),
        pltpu.make_async_copy(vel, vel_v, local_sem.at[5]),
    ]
    for copy in local:
        copy.start()

    for plane in range(4):
        fill = float(OUTSIDE) if plane == 3 else 0.0
        far1[plane] = jnp.full(far1.shape[1:], fill, f32)
        if plane < 3:
            far2[plane] = jnp.zeros(far2.shape[1:], f32)

    barrier = pltpu.get_barrier_semaphore()

    def greet(x, y):
        pl.semaphore_signal(barrier, inc=1, device_id=(sample, x, y), device_id_type=MESH)

    @pl.when(has_up)
    def _():
        greet(up, gy)
        greet(up, mate)

    @pl.when(has_down)
    def _():
        greet(down, gy)
        greet(down, mate)

    greet(gx, mate)

    def cut(value):
        return [value[:, j * LANES : (j + 1) * LANES] for j in PLACES]

    def put(target, plane, value):
        for j, piece in enumerate(cut(value)):
            for rows in (slice(0, ROWS), slice(ROWS, 2 * ROWS)):
                target[plane, j, rows, :] = piece

    for i in (1, 2, 3):
        local[i].wait()
    put(own1, 3, klass_v[...].astype(f32))
    put(own1, 0, disp_v[0])
    put(own1, 1, disp_v[1])
    put(own1, 2, pres_v[...])

    edge, rim = pl.ds(1 - gy, 1), pl.ds(RIM, 1)
    to_up = (pl.ds(0, REACH), pl.ds(ROWS, REACH))
    to_down = (pl.ds(ROWS - REACH, REACH), pl.ds(ROWS - REACH, REACH))
    routes = (
        (has_up, has_down, (sample, up, gy), to_up),
        (has_down, has_up, (sample, down, gy), to_down),
        (has_up, has_down, (sample, up, mate), to_up),
        (has_down, has_up, (sample, down, mate), to_down),
        (None, None, (sample, gx, mate), None),
    )
    STRAIGHT, CORNERS, ACROSS = (0, 1), (2, 3), (4,)
    messages = []

    def when(condition, act):
        if condition is None:
            act()
        else:
            pl.when(condition)(act)

    def send(own, far, planes, which, blocks=None):
        sent = []
        for n in which:
            going, coming, device, rows = routes[n]
            here, land = (edge, rim) if blocks is None else (blocks, blocks)
            if rows is None:
                source = own.at[planes, here, pl.ds(0, ROWS)]
                target = own.at[planes, land, pl.ds(0, ROWS)]
            else:
                source = own.at[planes, here, rows[0]]
                target = far.at[planes, land, rows[1]]
            m = len(messages)
            copy = pltpu.make_async_remote_copy(
                src_ref=source, dst_ref=target, send_sem=send_sem.at[m], recv_sem=recv_sem.at[m],
                device_id=device, device_id_type=MESH,
            )
            when(going, copy.start)
            messages.append((going, copy))
            sent.append((coming, copy))
        return sent

    waited = []

    def finish_sends(count):
        for going, copy in messages[len(waited) : count]:
            when(going, copy.wait_send)
            waited.append(copy)

    def arrive(sent):
        for coming, copy in sent:
            when(coming, copy.wait_recv)

    pl.semaphore_wait(
        barrier, 1 + 2 * has_up.astype(jnp.int32) + 2 * has_down.astype(jnp.int32)
    )
    fields, kinds = pl.ds(0, 3), pl.ds(3, 1)
    four = pl.ds(0, blocks)
    kinds_far = send(own1, far1, kinds, STRAIGHT, four) + send(own1, far1, kinds, CORNERS)
    kinds_rim = send(own1, far1, kinds, ACROSS)
    fields_far = send(own1, far1, fields, STRAIGHT, four) + send(own1, far1, fields, CORNERS)
    fields_rim = send(own1, far1, fields, ACROSS)

    sublane = lax.broadcasted_iota(jnp.int32, (ROWS, LANES), 0)
    lane = lax.broadcasted_iota(jnp.int32, (ROWS, LANES), 1)

    def mix(o, low, high, kind=f32):
        return kind(low) if low == high else jnp.where(sublane < ROWS - o, kind(low), kind(high))

    local[0].wait()

    def look_up(which, member):
        value = jnp.full(which.shape, table_s[table.shape[0] - 1, member], f32)
        for c in range(table.shape[0] - 1):
            value = jnp.where(which == c, table_s[c, member], value)
        return value

    classes = table.shape[0]
    for m in range(2):
        for c in range(classes):
            inverse[m, c] = 1.0 / jnp.full((ROWS, LANES), table_s[c, m], f32)

    def inverses(which):
        out = [jnp.full(which.shape, FAR, f32)] * 2
        for c in range(classes):
            chosen = which == float(c)
            out = [jnp.where(chosen, inverse[m, c], out[m]) for m in range(2)]
        return out

    for m, value in enumerate(inverses(own1[3, :blocks, 0:ROWS, :])):
        here_inv[m] = value

    klass_own = klass_v[...]
    for plane, member in ((0, 2), (1, 3)):
        for j, piece in enumerate(cut(look_up(klass_own, member))):
            still[plane, j] = piece
    local[4].wait()
    for j in range(blocks):
        words = [bits_v[w, :, PLACES[j] * LANES : (PLACES[j] + 1) * LANES] for w in range(bits.shape[0])]

        def broken(a, b):
            k = bond(a, b)
            return jnp.int32(1) if k is None else words[k // 12] & (1 << (k % 12))

        for own, w_to, v_to in ((True, w_own, v_own), (False, w_far, v_far)):
            for o, low, high in groups_of(own):
                for b in range(-columns_of(low, high), columns_of(low, high) + 1):
                    if (o, b) not in SLOTS[own]:
                        continue
                    n = SLOTS[own][o, b]
                    one = broken(low, b)
                    if o:
                        one = jnp.where(sublane < ROWS - o, one, broken(high, b))
                    squares = [a * a + b * b for a in (low, high)]
                    w_to[n, j] = jnp.where(one == 0, mix(o, *[2.0 / x**2 for x in squares]), 0.0)
                    v_to[n, j] = jnp.where(one == 0, mix(o, *[2.0 / x for x in squares]), 0.0)

    def load(get, which):
        runs = []
        for k in which:
            if runs and runs[-1][1] == k:
                runs[-1][1] = k + 1
            else:
                runs.append([k, k + 1])
        pieces = [get(*run) for run in runs]
        return pieces[0] if len(pieces) == 1 else jnp.concatenate(pieces, axis=0)

    def shift(get, b, outs=ALL):
        if b == 0:
            return load(get, outs)
        other = [(AFTER if b > 0 else BEFORE)[k] for k in outs]
        sources = sorted(set(outs) | set(other))
        turned = pltpu.roll(load(get, sources), (-b) % LANES, 2)

        def take(which):
            at = [sources.index(k) for k in which]
            return load(lambda i, j: turned[i:j], at)

        return jnp.where(lane < LANES - b if b > 0 else lane >= -b, take(outs), take(other))

    def tiles(own):
        top, bottom = slice(0, ROWS), slice(ROWS, 2 * ROWS)
        return [(top, (top, bottom))] if own else [(top, (top,)), (bottom, (bottom,))]

    valid = (lane < LANES // 2) == (gy == 0)

    def weigh(own, x):
        w_ref, v_ref, inv = (w_own, v_own, inv_own) if own else (w_far, v_far, inv_far)
        known = []
        for read, write in tiles(own):
            value = x[3, :, read, :]
            rim_value = jnp.where(valid, value[blocks:], float(OUTSIDE))
            known.append(inverses(jnp.concatenate([value[:blocks], rim_value], axis=0)))
        drain = jnp.zeros((blocks, ROWS, LANES), f32)
        for b in sorted(range(-REACH, REACH + 1), key=abs):
            for (read, write), pair in zip(tiles(own), known):
                for m, value in enumerate(pair):
                    moved = shift(lambda i, j: value[i:j], b)
                    for rows in write:
                        inv[m, b + REACH, :, rows, :] = moved
            for o, low, high in groups_of(own):
                if (o, b) not in SLOTS[own]:
                    continue
                n = SLOTS[own][o, b]
                cubes = [0.25 * math.sqrt(a * a + b * b) ** 3 for a in (low, high)]
                weight, flow = (
                    ref[n]
                    * pl.reciprocal(
                        here_inv[m] + inv[m, b + REACH, :, pl.ds(o, ROWS), :], approx=True
                    )
                    for m, ref in enumerate((w_ref, v_ref))
                )
                share = mix(o, *cubes) * weight
                w_ref[n] = weight
                v_ref[n] = flow - share
                drain = drain + (flow + share)
        return drain

    def centre(x):
        u, v, p = (x[plane, :blocks, 0:ROWS, :] for plane in range(3))
        for b in range(-REACH, REACH + 1):
            side_b[b + REACH] = float(b) * v + (0.25 * b * b) * p
        for own, target in ((True, ex_own), (False, ex_far)):
            for o, low, high in groups_of(own):
                here = mix(o, low, high) * u + mix(o, 0.25 * low * low, 0.25 * high * high) * p
                for b in range(-columns_of(low, high), columns_of(low, high) + 1):
                    if (o, b) in SLOTS[own]:
                        target[SLOTS[own][o, b]] = here if b == 0 else here + side_b[b + REACH]

    def evaluate(own, x, sums, outs=ALL, ready=False, ends="both"):
        w_ref, v_ref, ex, z, q_moved, y = (
            (w_own, v_own, ex_own, z_own, q_own, y_own)
            if own
            else (w_far, v_far, ex_far, z_far, q_far, y_far)
        )
        slots = SLOTS[own]
        force_x, force_y, gain = sums
        span = slice(outs[0], outs[-1] + 1)
        ready = ready or ends == "near"
        if not ready:
            for o, low, high in groups_of(own):
                if o:
                    rows = pl.ds(o, ROWS)
                    y[o - 1] = (
                        mix(o, low, high) * x[0, :, rows, :]
                        - mix(o, 0.25 * low * low, 0.25 * high * high) * x[2, :, rows, :]
                    )
        groups = groups_of(own)
        sets = (groups,) if len(outs) < len(ALL) else (groups[: HALF], groups[HALF:])
        for chosen in sets:
            row_sums = {}
            for b in range(REACH + 1):
                if not ready and chosen is sets[0]:
                    for read, write in tiles(own):
                        if b:
                            v, q = x[1, :, read, :], x[2, :, read, :]
                            bv, bq = float(b) * v, (-0.25 * b * b) * q
                            for rows in write:
                                z[REACH + b, :, rows, :] = bq + bv
                                z[REACH - b, :, rows, :] = bq - bv
                        for c in (b, -b) if b else (0,):
                            moved = shift(lambda i, j: x[2, i:j, read, :], c)
                            for rows in write:
                                q_moved[c + REACH, :, rows, :] = moved
                side_sum = None
                for o, low, high in chosen:
                    if (o, b) not in slots:
                        continue
                    rows = pl.ds(o, ROWS)

                    def one(c):
                        n = slots[o, c]

                        def there(i, j):
                            if c == 0:
                                return y[o - 1, i:j]
                            side = z[c + REACH, i:j, rows, :]
                            return side + y[o - 1, i:j] if o else side

                        if ends == "near":
                            return w_ref[n, span] * ex[n, span], None
                        far = shift(there, c, outs)
                        mag = w_ref[n, span] * (far - ex[n, span] if ends == "both" else far)
                        return mag, v_ref[n, span] * q_moved[c + REACH, span, rows, :]

                    def add(total, value):
                        return value if total is None else total + value

                    length = mix(o, *[math.sqrt(a * a + b * b) for a in (low, high)])
                    mag, flow = one(b)
                    if b:
                        mag2, flow2 = one(-b)
                        side_sum = add(side_sum, mag - mag2)
                        mag = mag + mag2
                    if o:
                        row_sums[o] = add(row_sums.get(o), mag)
                    if ends == "near":
                        gain = gain + length * mag
                        continue
                    gain = gain - length * mag + flow
                    if b:
                        gain = gain + flow2
                if side_sum is not None:
                    force_y = force_y - float(b) * side_sum if ends == "near" else force_y + float(b) * side_sum
            for o, low, high in chosen:
                if o:
                    part = mix(o, low, high) * row_sums[o]
                    force_x = force_x - part if ends == "near" else force_x + part
        return force_x, force_y, gain

    def duplicate_rim(x, planes):
        for plane in planes:
            x[plane, RIM, ROWS : 2 * ROWS, :] = x[plane, RIM, 0:ROWS, :]

    def finish(x, sums, drain, velocity, outs=ALL):
        span = slice(outs[0], outs[-1] + 1)
        force_x, force_y, gain = sums
        u0, u1, p = (x[plane, span, 0:ROWS, :] for plane in range(3))
        density, storage = still[0, span], still[1, span]
        v0 = velocity[0] + 0.1 * (density * force_x - 0.5 * velocity[0])
        v1 = velocity[1] + 0.1 * (density * force_y - 0.5 * velocity[1])
        pressure = p + 0.1 * storage * 0.1 * (gain - drain * p)
        return u0 + 0.1 * v0, u1 + 0.1 * v1, pressure, v0, v1

    zero = jnp.zeros((blocks, ROWS, LANES), f32)

    arrive(kinds_rim)
    duplicate_rim(own1, (3,))
    drain = weigh(True, own1)
    arrive(fields_rim)
    duplicate_rim(own1, (0, 1, 2))
    centre(own1)
    sums = evaluate(True, own1, (zero,) * 3)
    local[5].wait()
    velocity = [jnp.stack(cut(vel_v[i])) for i in range(2)]

    arrive(kinds_far)
    drain = drain + weigh(False, far1)
    arrive(fields_far)
    moving, after = [], []
    for outs in (OUTER, INNER):
        span = slice(outs[0], outs[-1] + 1)
        part = evaluate(False, far1, tuple(t[span] for t in sums), outs, outs != OUTER)
        new = finish(own1, part, drain[span], [t[span] for t in velocity], outs)
        for plane in range(3):
            own2[plane, span, 0:ROWS, :] = new[plane]
            own2[plane, span, ROWS : 2 * ROWS, :] = new[plane]
        after.append(new[3:])
        moving += send(own2, far2, fields, STRAIGHT, pl.ds(outs[0], len(outs)))
        if outs == OUTER:
            moving += send(own2, far2, fields, CORNERS)
            rim2 = send(own2, far2, fields, ACROSS)
    velocity = [jnp.concatenate(pair, axis=0) for pair in zip(*after)]

    arrive(rim2)
    duplicate_rim(own2, (0, 1, 2))
    centre(own2)
    sums = evaluate(True, own2, (zero,) * 3)
    sums = evaluate(False, None, sums, ends="near")
    finish_sends(len(messages) - 7)
    arrive(moving)
    sums = evaluate(False, far2, sums, ends="far")
    n0, n1, np_, v0, v1 = finish(own2, sums, drain, velocity)

    for k, j in enumerate(PLACES):
        at = slice(j * LANES, (j + 1) * LANES)
        out_disp[0, :, at] = n0[k]
        out_disp[1, :, at] = n1[k]
        out_vel[0, :, at] = v0[k]
        out_vel[1, :, at] = v1[k]
        out_pres[:, at] = np_[k]

    finish_sends(len(messages))


def hand_over(a, b, c, out_a, out_b, out_c, sems):
    copies = [
        pltpu.make_async_copy(source, target, sems.at[i])
        for i, (source, target) in enumerate(((a, out_a), (b, out_b), (c, out_c)))
    ]
    for copy in copies:
        copy.start()
    for copy in copies:
        copy.wait()


def body(gx_count, displacement, velocity, pressure, broken_bits, material_class, table):
    height, breadth = pressure.shape
    assert height == ROWS and breadth % LANES == 0 and breadth == len(PLACES) * LANES
    blocks = breadth // LANES
    vmem = pl.BlockSpec(memory_space=pltpu.VMEM)
    anywhere = pl.BlockSpec(memory_space=pltpu.HBM)
    f, i32 = jnp.float32, jnp.int32
    dma = pltpu.SemaphoreType.DMA
    n_own, n_far = (len(SLOTS[own]) for own in (True, False))

    def planes(n, blocks, rows):
        return pltpu.VMEM((n, blocks, rows, LANES), f)

    shapes = (displacement.shape, velocity.shape, pressure.shape)
    results = pl.pallas_call(
        functools.partial(kernel, gx_count),
        out_shape=tuple(pltpu.VMEM(s, f) for s in shapes),
        in_specs=[anywhere] * 6,
        out_specs=(vmem, vmem, vmem),
        scratch_shapes=[
            pltpu.VMEM(displacement.shape, f),
            pltpu.VMEM(velocity.shape, f),
            pltpu.VMEM(pressure.shape, f),
            pltpu.VMEM(broken_bits.shape, i32),
            pltpu.VMEM(material_class.shape, i32),
            pltpu.SMEM(table.shape, f),
            planes(4, blocks + 1, 2 * ROWS),
            planes(4, blocks + 1, 2 * ROWS),
            planes(3, blocks + 1, 2 * ROWS),
            planes(3, blocks + 1, 2 * ROWS),
            planes(SPAN, blocks + 1, 2 * ROWS),
            planes(SPAN, blocks + 1, 2 * ROWS),
            planes(SPAN, blocks, 2 * ROWS),
            planes(SPAN, blocks, 2 * ROWS),
            pltpu.VMEM((2, SPAN, blocks, 2 * ROWS, LANES), f),
            pltpu.VMEM((2, SPAN, blocks, 2 * ROWS, LANES), f),
            planes(2, table.shape[0], ROWS),
            planes(2, blocks, ROWS),
            planes(n_own, blocks, ROWS),
            planes(n_own, blocks, ROWS),
            planes(n_far, blocks, ROWS),
            planes(n_far, blocks, ROWS),
            planes(n_own, blocks, ROWS),
            planes(n_far, blocks, ROWS),
            planes(ROWS - 1, blocks + 1, ROWS),
            planes(ROWS - 1, blocks + 1, ROWS),
            planes(SPAN, blocks, ROWS),
            planes(2, blocks, ROWS),
            dma((6,)), dma((MESSAGES,)), dma((MESSAGES,)),
        ],
        compiler_params=pltpu.CompilerParams(
            collective_id=0, has_side_effects=True, vmem_limit_bytes=62 * 1024 * 1024
        ),
        name="peridynamics",
    )(displacement, velocity, pressure, broken_bits, material_class, table)
    return pl.pallas_call(
        hand_over,
        out_shape=tuple(jax.ShapeDtypeStruct(s, f) for s in shapes),
        in_specs=[vmem] * 3,
        out_specs=(anywhere,) * 3,
        scratch_shapes=[dma((3,))],
        name="hand_over",
    )(*[pltpu.with_memory_space_constraint(r, pltpu.VMEM) for r in results])


def solution(mesh):
    plane = P(("sample", "gx"), "gy")
    stack = P(None, ("sample", "gx"), "gy")
    assert mesh.shape["gy"] == 2
    return jax.shard_map(
        functools.partial(body, mesh.shape["gx"]),
        mesh=mesh,
        in_specs=(stack, stack, plane, stack, plane, P("sample", None)),
        out_specs=(stack, stack, plane),
        check_vma=False,
    )
```

time: 14.1 us -> 13.6 us (0.965)
  Pallas kernels: 13.3 us -> 12.8 us
    pallas_call x1, Pallas kernels: 12.7 us -> 12.2 us  [body(): pl.pallas_call(functools.partial(kernel, gx_count), out_shape=tuple((pltp...]
where the time goes in v2:
time: 13.6 us; the launch traced here: 13.5 us
  Pallas kernels  12.8 us (94%)
  between operations  0.64 us (5%)
    pallas_call x1, Pallas kernels, body(): pl.pallas_call(functools.partial(kernel, gx_count), out_shape=tuple((pltp...  12.2 us
    pallas_call x1, Pallas kernels, body(): pl.pallas_call(hand_over, out_shape=tuple((jax.ShapeDtypeStruct(s, f) for...  0.66 us

profile of v2, /device:TPU:0, one launch (start us, length us, event | category | flops | bytes accessed | tf_op | source)
XLA Modules:
  0.0 13.5 jit_solution(844333726445562351)
XLA Ops:
  0.6 12.2 %peridynamics.1 = (f32[2,8,512]{2,1,0:T(8,128)S(1)}, f32[2,8,512]{2,1,0:T(8,128)S(1)}, f32[8,512]{1,0:T(8,128)S(1)}) custom-call(f32[2,8,512]{2,1,0:T(8,128)} %disp.1, f32[2,8,512]{2,1,0:T(8,128)} %vel.1, f32[8,512]{1,0:T(8,128)} %pres.1, s32[10,8,512]{2,1,0:T(8,128)} %bits.1, s32[8,512]{1,0:T(8,128)} %klass.1, f32[4,4]{1,0:T(4,128)} %table.1), custom_call_target="tpu_custom_call" | custom-call | tf_op jit(solution)/shard_map/peridynamics/pallas_call | solution.py:485
  12.8 0.7 %hand_over.1 = (f32[2,8,512]{2,1,0:T(8,128)}, f32[2,8,512]{2,1,0:T(8,128)}, f32[8,512]{1,0:T(8,128)}) custom-call(f32[2,8,512]{2,1,0:T(8,128)S(1)} %get-tuple-element.6.a, f32[2,8,512]{2,1,0:T(8,128)S(1)} %get-tuple-element.7.b, f32[8,512]{1,0:T(8,128)S(1)} %get-tuple-element.8.c), custom_call_target="tpu_custom_call" | custom-call | tf_op jit(solution)/shard_map/hand_over/pallas_call | solution.py:526

commit v3 on v2

--- a/solution.py
+++ b/solution.py
@@ -18,7 +18,8 @@
 RIM = len(PLACES)
 AFTER, BEFORE = (2, RIM, 3, 1), (RIM, 3, 0, 2)
 OUTER, INNER, ALL = (0, 1), (2, 3), (0, 1, 2, 3)
-MESSAGES = 17
+MESSAGES = 14
+STRIP = 16
 HALF = 4
 FAR = 3.0e38
 
@@ -63,7 +64,7 @@
     gx_count, disp, vel, pres, bits, klass, table,
     out_disp, out_vel, out_pres,
     disp_v, vel_v, pres_v, bits_v, klass_v, table_s,
-    own1, far1, own2, far2,
+    own1, far1, own2, far2, own_pack, far_pack,
     z_own, z_far, q_own, q_far, inv_own, inv_far, inverse, here_inv,
     w_own, v_own, w_far, v_far, ex_own, ex_far, y_own, y_far, side_b, still,
     local_sem, send_sem, recv_sem,
@@ -91,6 +92,7 @@
         far1[plane] = jnp.full(far1.shape[1:], fill, f32)
         if plane < 3:
             far2[plane] = jnp.zeros(far2.shape[1:], f32)
+    far_pack[...] = jnp.full(far_pack.shape, float(OUTSIDE), f32)
 
     barrier = pltpu.get_barrier_semaphore()
 
@@ -143,20 +145,37 @@
         else:
             pl.when(condition)(act)
 
-    def send(own, far, planes, which, blocks=None):
+    sublane = lax.broadcasted_iota(jnp.int32, (ROWS, LANES), 0)
+    lane = lax.broadcasted_iota(jnp.int32, (ROWS, LANES), 1)
+
+    def pack(x, planes, which):
+        strip = ((lane - (1 - gy) * (LANES - STRIP)) & (LANES - 1)) >> 4
+        total = None
+        for plane in range(planes):
+            value = x[plane, pl.ds(1 - gy, 1), 0:ROWS, :][0]
+            if plane:
+                total = jnp.where(strip == plane, pltpu.roll(value, STRIP * plane, 1), total)
+            else:
+                total = value
+        own_pack[which] = total
+
+    def unpack(x, planes, which):
+        for rows in (slice(0, ROWS), slice(ROWS, 2 * ROWS)):
+            value = far_pack[which, rows, :]
+            for plane in range(planes):
+                x[plane, RIM, rows, :] = (
+                    pltpu.roll(value, LANES - STRIP * plane, 1) if plane else value
+                )
+
+    def send(routes_used, source, target):
         sent = []
-        for n in which:
+        for n in routes_used:
             going, coming, device, rows = routes[n]
-            here, land = (edge, rim) if blocks is None else (blocks, blocks)
-            if rows is None:
-                source = own.at[planes, here, pl.ds(0, ROWS)]
-                target = own.at[planes, land, pl.ds(0, ROWS)]
-            else:
-                source = own.at[planes, here, rows[0]]
-                target = far.at[planes, land, rows[1]]
+            here, there = (pl.ds(0, ROWS),) * 2 if rows is None else rows
             m = len(messages)
             copy = pltpu.make_async_remote_copy(
-                src_ref=source, dst_ref=target, send_sem=send_sem.at[m], recv_sem=recv_sem.at[m],
+                src_ref=source(here), dst_ref=target(there),
+                send_sem=send_sem.at[m], recv_sem=recv_sem.at[m],
                 device_id=device, device_id_type=MESH,
             )
             when(going, copy.start)
@@ -164,6 +183,17 @@
             sent.append((coming, copy))
         return sent
 
+    def send_straight(own, far, planes, blocks):
+        return send(
+            STRAIGHT, lambda r: own.at[planes, blocks, r], lambda r: far.at[planes, blocks, r]
+        )
+
+    def send_across(own):
+        return send(ACROSS, lambda r: own.at[:, edge, r], lambda r: own.at[:, rim, r])
+
+    def send_corners(which):
+        return send(CORNERS, lambda r: own_pack.at[which, r], lambda r: far_pack.at[which, r])
+
     waited = []
 
     def finish_sends(count):
@@ -175,18 +205,16 @@
         for coming, copy in sent:
             when(coming, copy.wait_recv)
 
+    pack(own1, 4, 0)
     pl.semaphore_wait(
         barrier, 1 + 2 * has_up.astype(jnp.int32) + 2 * has_down.astype(jnp.int32)
     )
     fields, kinds = pl.ds(0, 3), pl.ds(3, 1)
     four = pl.ds(0, blocks)
-    kinds_far = send(own1, far1, kinds, STRAIGHT, four) + send(own1, far1, kinds, CORNERS)
-    kinds_rim = send(own1, far1, kinds, ACROSS)
-    fields_far = send(own1, far1, fields, STRAIGHT, four) + send(own1, far1, fields, CORNERS)
-    fields_rim = send(own1, far1, fields, ACROSS)
-
-    sublane = lax.broadcasted_iota(jnp.int32, (ROWS, LANES), 0)
-    lane = lax.broadcasted_iota(jnp.int32, (ROWS, LANES), 1)
+    four = pl.ds(0, blocks)
+    kinds_far = send_straight(own1, far1, kinds, four) + send_corners(0)
+    fields_far = send_straight(own1, far1, fields, four)
+    rim1 = send_across(own1)
 
     def mix(o, low, high, kind=f32):
         return kind(low) if low == high else jnp.where(sublane < ROWS - o, kind(low), kind(high))
@@ -408,17 +436,16 @@
 
     zero = jnp.zeros((blocks, ROWS, LANES), f32)
 
-    arrive(kinds_rim)
-    duplicate_rim(own1, (3,))
+    arrive(rim1)
+    duplicate_rim(own1, range(4))
     drain = weigh(True, own1)
-    arrive(fields_rim)
-    duplicate_rim(own1, (0, 1, 2))
     centre(own1)
     sums = evaluate(True, own1, (zero,) * 3)
     local[5].wait()
     velocity = [jnp.stack(cut(vel_v[i])) for i in range(2)]
 
     arrive(kinds_far)
+    unpack(far1, 4, 0)
     drain = drain + weigh(False, far1)
     arrive(fields_far)
     moving, after = [], []
@@ -430,19 +457,21 @@
             own2[plane, span, 0:ROWS, :] = new[plane]
             own2[plane, span, ROWS : 2 * ROWS, :] = new[plane]
         after.append(new[3:])
-        moving += send(own2, far2, fields, STRAIGHT, pl.ds(outs[0], len(outs)))
+        moving += send_straight(own2, far2, fields, pl.ds(outs[0], len(outs)))
         if outs == OUTER:
-            moving += send(own2, far2, fields, CORNERS)
-            rim2 = send(own2, far2, fields, ACROSS)
+            pack(own2, 3, 1)
+            moving += send_corners(1)
+            rim2 = send_across(own2)
     velocity = [jnp.concatenate(pair, axis=0) for pair in zip(*after)]
 
     arrive(rim2)
-    duplicate_rim(own2, (0, 1, 2))
+    duplicate_rim(own2, range(3))
     centre(own2)
     sums = evaluate(True, own2, (zero,) * 3)
     sums = evaluate(False, None, sums, ends="near")
     finish_sends(len(messages) - 7)
     arrive(moving)
+    unpack(far2, 3, 1)
     sums = evaluate(False, far2, sums, ends="far")
     n0, n1, np_, v0, v1 = finish(own2, sums, drain, velocity)
 
@@ -498,6 +527,8 @@
             planes(4, blocks + 1, 2 * ROWS),
             planes(3, blocks + 1, 2 * ROWS),
             planes(3, blocks + 1, 2 * ROWS),
+            pltpu.VMEM((2, ROWS, LANES), f),
+            pltpu.VMEM((2, 2 * ROWS, LANES), f),
             planes(SPAN, blocks + 1, 2 * ROWS),
             planes(SPAN, blocks + 1, 2 * ROWS),
             planes(SPAN, blocks, 2 * ROWS),

time: 13.6 us -> 13.5 us (level)
  no operation moved by 1% of the time
where the time goes in v3:
time: 13.5 us; the launch traced here: 13.4 us
  Pallas kernels  12.7 us (94%)
  between operations  0.64 us (5%)
    pallas_call x1, Pallas kernels, body(): pl.pallas_call(functools.partial(kernel, gx_count), out_shape=tuple((pltp...  12.1 us
    pallas_call x1, Pallas kernels, body(): pl.pallas_call(hand_over, out_shape=tuple((jax.ShapeDtypeStruct(s, f) for...  0.66 us

profile of v3, /device:TPU:0, one launch (start us, length us, event | category | flops | bytes accessed | tf_op | source)
XLA Modules:
  0.0 13.4 jit_solution(16376512068327350423)
XLA Ops:
  0.6 12.1 %peridynamics.1 = (f32[2,8,512]{2,1,0:T(8,128)S(1)}, f32[2,8,512]{2,1,0:T(8,128)S(1)}, f32[8,512]{1,0:T(8,128)S(1)}) custom-call(f32[2,8,512]{2,1,0:T(8,128)} %disp.1, f32[2,8,512]{2,1,0:T(8,128)} %vel.1, f32[8,512]{1,0:T(8,128)} %pres.1, s32[10,8,512]{2,1,0:T(8,128)} %bits.1, s32[8,512]{1,0:T(8,128)} %klass.1, f32[4,4]{1,0:T(4,128)} %table.1), custom_call_target="tpu_custom_call" | custom-call | tf_op jit(solution)/shard_map/peridynamics/pallas_call | solution.py:514
  12.7 0.7 %hand_over.1 = (f32[2,8,512]{2,1,0:T(8,128)}, f32[2,8,512]{2,1,0:T(8,128)}, f32[8,512]{1,0:T(8,128)}) custom-call(f32[2,8,512]{2,1,0:T(8,128)S(1)} %get-tuple-element.6.a, f32[2,8,512]{2,1,0:T(8,128)S(1)} %get-tuple-element.7.b, f32[8,512]{1,0:T(8,128)S(1)} %get-tuple-element.8.c), custom_call_target="tpu_custom_call" | custom-call | tf_op jit(solution)/shard_map/hand_over/pallas_call | solution.py:557

commit v4 on v3

--- a/solution.py
+++ b/solution.py
@@ -21,6 +21,8 @@
 MESSAGES = 14
 STRIP = 16
 HALF = 4
+JOINED = (1, 2, 3)
+Y_SLOTS = ROWS + len(JOINED)
 FAR = 3.0e38
 
 half_width = {a: math.isqrt(37 - a * a) for a in range(-REACH, REACH + 1)}
@@ -38,10 +40,9 @@
 
 
 def groups_of(own):
-    out = [(0, 0, 0)] if own else []
-    for o in range(1, ROWS):
-        out.append((o, o, o - ROWS) if own else (o, o - ROWS, o))
-    return out
+    offsets = range(ROWS) if own else range(2, ROWS - 1)
+    out = [(o, o, o - ROWS if o else 0) if own else (o, o - ROWS, o) for o in offsets]
+    return out if own else out + [(-m, -m, m) for m in JOINED]
 
 
 def columns_of(low, high):
@@ -51,8 +52,14 @@
 def slots_of(own):
     slots = {}
     for o, low, high in groups_of(own):
-        for b in range(-columns_of(low, high), columns_of(low, high) + 1):
-            if (o, b) != (0, 0):
+        widths = half_width.get(low, -1), half_width.get(high, -1)
+        for b in range(-max(widths), max(widths) + 1):
+            one_sided = abs(b) > min(widths)
+            if not own and o > 0 and one_sided:
+                continue
+            if o < 0 and abs(b) <= half_width.get(ROWS + o, -1):
+                continue
+            if low or b:
                 slots[o, b] = len(slots)
     return slots
 
@@ -216,8 +223,16 @@
     fields_far = send_straight(own1, far1, fields, four)
     rim1 = send_across(own1)
 
+    def first_rows(o):
+        return sublane < (ROWS - o if o >= 0 else -o)
+
     def mix(o, low, high, kind=f32):
-        return kind(low) if low == high else jnp.where(sublane < ROWS - o, kind(low), kind(high))
+        return kind(low) if low == high else jnp.where(first_rows(o), kind(low), kind(high))
+
+    def window(get, o):
+        if o >= 0:
+            return get(pl.ds(o, ROWS))
+        return jnp.where(first_rows(o), get(pl.ds(ROWS + o, ROWS)), get(pl.ds(-o, ROWS)))
 
     local[0].wait()
 
@@ -261,8 +276,10 @@
                         continue
                     n = SLOTS[own][o, b]
                     one = broken(low, b)
-                    if o:
-                        one = jnp.where(sublane < ROWS - o, one, broken(high, b))
+                    if low != high:
+                        one = jnp.where(first_rows(o), one, broken(high, b))
+                    if o < 0:
+                        one = jnp.where((sublane >= -o) & (sublane < ROWS + o), 1, one)
                     squares = [a * a + b * b for a in (low, high)]
                     w_to[n, j] = jnp.where(one == 0, mix(o, *[2.0 / x**2 for x in squares]), 0.0)
                     v_to[n, j] = jnp.where(one == 0, mix(o, *[2.0 / x for x in squares]), 0.0)
@@ -318,7 +335,8 @@
                 weight, flow = (
                     ref[n]
                     * pl.reciprocal(
-                        here_inv[m] + inv[m, b + REACH, :, pl.ds(o, ROWS), :], approx=True
+                        here_inv[m] + window(lambda r: inv[m, b + REACH, :, r, :], o),
+                        approx=True,
                     )
                     for m, ref in enumerate((w_ref, v_ref))
                 )
@@ -351,11 +369,11 @@
         ready = ready or ends == "near"
         if not ready:
             for o, low, high in groups_of(own):
-                if o:
-                    rows = pl.ds(o, ROWS)
-                    y[o - 1] = (
-                        mix(o, low, high) * x[0, :, rows, :]
-                        - mix(o, 0.25 * low * low, 0.25 * high * high) * x[2, :, rows, :]
+                if low:
+                    u, q = (window(lambda r: x[m, :, r, :], o) for m in (0, 2))
+                    y[o % Y_SLOTS] = (
+                        mix(o, low, high) * u
+                        - mix(o, 0.25 * low * low, 0.25 * high * high) * q
                     )
         groups = groups_of(own)
         sets = (groups,) if len(outs) < len(ALL) else (groups[: HALF], groups[HALF:])
@@ -378,22 +396,21 @@
                 for o, low, high in chosen:
                     if (o, b) not in slots:
                         continue
-                    rows = pl.ds(o, ROWS)
-
                     def one(c):
                         n = slots[o, c]
 
                         def there(i, j):
                             if c == 0:
-                                return y[o - 1, i:j]
-                            side = z[c + REACH, i:j, rows, :]
-                            return side + y[o - 1, i:j] if o else side
+                                return y[o % Y_SLOTS, i:j]
+                            side = window(lambda r: z[c + REACH, i:j, r, :], o)
+                            return side + y[o % Y_SLOTS, i:j] if low else side
 
                         if ends == "near":
                             return w_ref[n, span] * ex[n, span], None
                         far = shift(there, c, outs)
                         mag = w_ref[n, span] * (far - ex[n, span] if ends == "both" else far)
-                        return mag, v_ref[n, span] * q_moved[c + REACH, span, rows, :]
+                        moved = window(lambda r: q_moved[c + REACH, span, r, :], o)
+                        return mag, v_ref[n, span] * moved
 
                     def add(total, value):
                         return value if total is None else total + value
@@ -404,7 +421,7 @@
                         mag2, flow2 = one(-b)
                         side_sum = add(side_sum, mag - mag2)
                         mag = mag + mag2
-                    if o:
+                    if low:
                         row_sums[o] = add(row_sums.get(o), mag)
                     if ends == "near":
                         gain = gain + length * mag
@@ -415,7 +432,7 @@
                 if side_sum is not None:
                     force_y = force_y - float(b) * side_sum if ends == "near" else force_y + float(b) * side_sum
             for o, low, high in chosen:
-                if o:
+                if low:
                     part = mix(o, low, high) * row_sums[o]
                     force_x = force_x - part if ends == "near" else force_x + part
         return force_x, force_y, gain
@@ -543,8 +560,8 @@
             planes(n_far, blocks, ROWS),
             planes(n_own, blocks, ROWS),
             planes(n_far, blocks, ROWS),
-            planes(ROWS - 1, blocks + 1, ROWS),
-            planes(ROWS - 1, blocks + 1, ROWS),
+            planes(Y_SLOTS, blocks + 1, ROWS),
+            planes(Y_SLOTS, blocks + 1, ROWS),
             planes(SPAN, blocks, ROWS),
             planes(2, blocks, ROWS),
             dma((6,)), dma((MESSAGES,)), dma((MESSAGES,)),

time: 13.5 us -> 13.2 us (0.978)
  Pallas kernels: 12.7 us -> 12.4 us
    pallas_call x1, Pallas kernels: 12.1 us -> 11.7 us  [body(): pl.pallas_call(functools.partial(kernel, gx_count), out_shape=tuple((pltp...]
where the time goes in v4:
time: 13.2 us; the launch traced here: 13 us
  Pallas kernels  12.4 us (94%)
  between operations  0.64 us (5%)
    pallas_call x1, Pallas kernels, body(): pl.pallas_call(functools.partial(kernel, gx_count), out_shape=tuple((pltp...  11.7 us
    pallas_call x1, Pallas kernels, body(): pl.pallas_call(hand_over, out_shape=tuple((jax.ShapeDtypeStruct(s, f) for...  0.66 us

profile of v4, /device:TPU:0, one launch (start us, length us, event | category | flops | bytes accessed | tf_op | source)
XLA Modules:
  0.0 13.0 jit_solution(7958008565280399001)
XLA Ops:
  0.6 11.7 %peridynamics.1 = (f32[2,8,512]{2,1,0:T(8,128)S(1)}, f32[2,8,512]{2,1,0:T(8,128)S(1)}, f32[8,512]{1,0:T(8,128)S(1)}) custom-call(f32[2,8,512]{2,1,0:T(8,128)} %disp.1, f32[2,8,512]{2,1,0:T(8,128)} %vel.1, f32[8,512]{1,0:T(8,128)} %pres.1, s32[10,8,512]{2,1,0:T(8,128)} %bits.1, s32[8,512]{1,0:T(8,128)} %klass.1, f32[4,4]{1,0:T(4,128)} %table.1), custom_call_target="tpu_custom_call" | custom-call | tf_op jit(solution)/shard_map/peridynamics/pallas_call | solution.py:531
  12.4 0.7 %hand_over.1 = (f32[2,8,512]{2,1,0:T(8,128)}, f32[2,8,512]{2,1,0:T(8,128)}, f32[8,512]{1,0:T(8,128)}) custom-call(f32[2,8,512]{2,1,0:T(8,128)S(1)} %get-tuple-element.6.a, f32[2,8,512]{2,1,0:T(8,128)S(1)} %get-tuple-element.7.b, f32[8,512]{1,0:T(8,128)S(1)} %get-tuple-element.8.c), custom_call_target="tpu_custom_call" | custom-call | tf_op jit(solution)/shard_map/hand_over/pallas_call | solution.py:574

commit v5 on v4

--- a/solution.py
+++ b/solution.py
@@ -21,8 +21,8 @@
 MESSAGES = 14
 STRIP = 16
 HALF = 4
-JOINED = (1, 2, 3)
-Y_SLOTS = ROWS + len(JOINED)
+JOINED = (2, 3)
+Y_SLOTS = ROWS + 3
 FAR = 3.0e38
 
 half_width = {a: math.isqrt(37 - a * a) for a in range(-REACH, REACH + 1)}
@@ -43,6 +43,9 @@
     offsets = range(ROWS) if own else range(2, ROWS - 1)
     out = [(o, o, o - ROWS if o else 0) if own else (o, o - ROWS, o) for o in offsets]
     return out if own else out + [(-m, -m, m) for m in JOINED]
+
+
+RING = 16
 
 
 def columns_of(low, high):
@@ -74,6 +77,7 @@
     own1, far1, own2, far2, own_pack, far_pack,
     z_own, z_far, q_own, q_far, inv_own, inv_far, inverse, here_inv,
     w_own, v_own, w_far, v_far, ex_own, ex_far, y_own, y_far, side_b, still,
+    ring1, ring2, ring_here, w_ring, v_ring, spread,
     local_sem, send_sem, recv_sem,
 ):
     f32 = jnp.float32
@@ -320,6 +324,13 @@
             value = x[3, :, read, :]
             rim_value = jnp.where(valid, value[blocks:], float(OUTSIDE))
             known.append(inverses(jnp.concatenate([value[:blocks], rim_value], axis=0)))
+        if not own:
+            for m in range(2):
+                top, bottom = known[0][m], known[1][m]
+                for i, k in enumerate(spots):
+                    at = slice(2 * i, 2 * i + 1)
+                    ring1[3 + m, at, :] = top[k, ROWS - 1 : ROWS]
+                    ring1[3 + m, 2 * i + 1 : 2 * i + 2, :] = bottom[k, 0:1]
         drain = jnp.zeros((blocks, ROWS, LANES), f32)
         for b in sorted(range(-REACH, REACH + 1), key=abs):
             for (read, write), pair in zip(tiles(own), known):
@@ -451,12 +462,108 @@
         pressure = p + 0.1 * storage * 0.1 * (gain - drain * p)
         return u0 + 0.1 * v0, u1 + 0.1 * v1, pressure, v0, v1
 
+    spots = [RIM] + [PLACES.index(j) for j in range(blocks)] + [RIM]
+    odd = (sublane & 1) == 1
+    step_a = jnp.where(odd, 1.0, -1.0)
+
+    def fill_ring(ring, plane, get):
+        for i, k in enumerate(spots):
+            ring[plane, 2 * i : 2 * i + 1, :] = get(k, ROWS - 1)
+            ring[plane, 2 * i + 1 : 2 * i + 2, :] = get(k, ROWS)
+
+    def ring_fields(ring, far):
+        for plane in range(3):
+            fill_ring(ring, plane, lambda k, r: far[plane, k, r : r + 1, :])
+
+    def ring_centre(plane, get):
+        for j in range(blocks):
+            k = PLACES.index(j)
+            ring_here[plane, 2 * j : 2 * j + 1, :] = get(k, 0)
+            ring_here[plane, 2 * j + 1 : 2 * j + 2, :] = get(k, ROWS - 1)
+
+    def ring_masks():
+        for b in range(-REACH, REACH + 1):
+            for ref, scale in ((w_ring, 2.0 / (1 + b * b) ** 2), (v_ring, 2.0 / (1 + b * b))):
+                for j in range(blocks):
+                    for i, (a, r) in enumerate(((-1, 0), (1, ROWS - 1))):
+                        k = bond(a, b)
+                        word = bits_v[k // 12, r : r + 1, j * LANES : (j + 1) * LANES]
+                        ref[b + REACH, 2 * j + i : 2 * j + i + 1, :] = jnp.where(
+                            (word & (1 << (k % 12))) == 0, scale, 0.0
+                        )
+
+    MAIN = pl.ds(2, ROWS)
+
+    def ring_shift(get, b):
+        if b == 0:
+            return get(MAIN)
+        other = pl.ds(4, ROWS) if b > 0 else pl.ds(0, ROWS)
+        mine, next_to = (pltpu.roll(get(r), (-b) % LANES, 1) for r in (MAIN, other))
+        return jnp.where(lane < LANES - b if b > 0 else lane >= -b, mine, next_to)
+
+    def ring_weigh():
+        drain = jnp.zeros((ROWS, LANES), f32)
+        for b in range(-REACH, REACH + 1):
+            weight, flow = (
+                ref[b + REACH]
+                * pl.reciprocal(
+                    ring_here[3 + m] + ring_shift(lambda r: ring1[3 + m, r, :], b), approx=True
+                )
+                for m, ref in enumerate((w_ring, v_ring))
+            )
+            share = (0.25 * math.sqrt(1 + b * b) ** 3) * weight
+            w_ring[b + REACH] = weight
+            v_ring[b + REACH] = flow - share
+            drain = drain + (flow + share)
+        return drain
+
+    def ring_sums(ring):
+        u, v, p = (ring_here[plane] for plane in range(3))
+        near = step_a * u + 0.25 * p
+        force_x = force_y = gain = pull = jnp.zeros((ROWS, LANES), f32)
+        for b in range(-REACH, REACH + 1):
+            def there(r):
+                value = step_a * ring[0, r, :] - (0.25 + 0.25 * b * b) * ring[2, r, :]
+                return value + float(b) * ring[1, r, :] if b else value
+
+            mine = near + (float(b) * v + (0.25 * b * b) * p) if b else near
+            mag = w_ring[b + REACH] * (ring_shift(there, b) - mine)
+            gain = gain + v_ring[b + REACH] * ring_shift(lambda r: ring[2, r, :], b)
+            pull = pull + math.sqrt(1 + b * b) * mag
+            force_x = force_x + mag
+            force_y = force_y + float(b) * mag
+        return step_a * force_x, force_y, gain - pull
+
+    def unring(values):
+        out = []
+        for i, value in enumerate(values):
+            spread[i] = value
+            parts = []
+            for j in PLACES:
+                first, last = (
+                    jnp.broadcast_to(spread[i, 2 * j + e : 2 * j + e + 1, :], (ROWS, LANES))
+                    for e in (0, 1)
+                )
+                parts.append(
+                    jnp.where(sublane == 0, first, jnp.where(sublane == ROWS - 1, last, 0.0))
+                )
+            out.append(jnp.stack(parts))
+        return out
+
+    def with_ring(sums, ring):
+        return tuple(t + r for t, r in zip(sums, unring(ring_sums(ring))))
+
     zero = jnp.zeros((blocks, ROWS, LANES), f32)
 
     arrive(rim1)
     duplicate_rim(own1, range(4))
     drain = weigh(True, own1)
     centre(own1)
+    ring_masks()
+    for plane in range(3):
+        ring_centre(plane, lambda k, r: own1[plane, k, r : r + 1, :])
+    for m in range(2):
+        ring_centre(3 + m, lambda k, r: here_inv[m, k, r : r + 1, :])
     sums = evaluate(True, own1, (zero,) * 3)
     local[5].wait()
     velocity = [jnp.stack(cut(vel_v[i])) for i in range(2)]
@@ -464,18 +571,20 @@
     arrive(kinds_far)
     unpack(far1, 4, 0)
     drain = drain + weigh(False, far1)
+    drain = drain + unring([ring_weigh()])[0]
     arrive(fields_far)
+    ring_fields(ring1, far1)
     moving, after = [], []
-    for outs in (OUTER, INNER):
+    for outs in (ALL,):
         span = slice(outs[0], outs[-1] + 1)
-        part = evaluate(False, far1, tuple(t[span] for t in sums), outs, outs != OUTER)
+        part = with_ring(evaluate(False, far1, sums), ring1)
         new = finish(own1, part, drain[span], [t[span] for t in velocity], outs)
         for plane in range(3):
             own2[plane, span, 0:ROWS, :] = new[plane]
             own2[plane, span, ROWS : 2 * ROWS, :] = new[plane]
         after.append(new[3:])
         moving += send_straight(own2, far2, fields, pl.ds(outs[0], len(outs)))
-        if outs == OUTER:
+        if True:
             pack(own2, 3, 1)
             moving += send_corners(1)
             rim2 = send_across(own2)
@@ -486,10 +595,14 @@
     centre(own2)
     sums = evaluate(True, own2, (zero,) * 3)
     sums = evaluate(False, None, sums, ends="near")
-    finish_sends(len(messages) - 7)
+    for plane in range(3):
+        ring_centre(plane, lambda k, r: own2[plane, k, r : r + 1, :])
+    finish_sends(7)
     arrive(moving)
     unpack(far2, 3, 1)
+    ring_fields(ring2, far2)
     sums = evaluate(False, far2, sums, ends="far")
+    sums = with_ring(sums, ring2)
     n0, n1, np_, v0, v1 = finish(own2, sums, drain, velocity)
 
     for k, j in enumerate(PLACES):
@@ -564,6 +677,12 @@
             planes(Y_SLOTS, blocks + 1, ROWS),
             planes(SPAN, blocks, ROWS),
             planes(2, blocks, ROWS),
+            pltpu.VMEM((5, RING, LANES), f),
+            pltpu.VMEM((5, RING, LANES), f),
+            pltpu.VMEM((5, ROWS, LANES), f),
+            pltpu.VMEM((SPAN, ROWS, LANES), f),
+            pltpu.VMEM((SPAN, ROWS, LANES), f),
+            pltpu.VMEM((3, ROWS, LANES), f),
             dma((6,)), dma((MESSAGES,)), dma((MESSAGES,)),
         ],
         compiler_params=pltpu.CompilerParams(

time: 13.2 us -> 13 us (0.985)
  Pallas kernels: 12.4 us -> 12.2 us
    pallas_call x1, Pallas kernels: 11.7 us -> 11.6 us  [body(): pl.pallas_call(functools.partial(kernel, gx_count), out_shape=tuple((pltp...]
where the time goes in v5:
time: 13 us; the launch traced here: 12.9 us
  Pallas kernels  12.2 us (94%)
  between operations  0.64 us (5%)
    pallas_call x1, Pallas kernels, body(): pl.pallas_call(functools.partial(kernel, gx_count), out_shape=tuple((pltp...  11.6 us
    pallas_call x1, Pallas kernels, body(): pl.pallas_call(hand_over, out_shape=tuple((jax.ShapeDtypeStruct(s, f) for...  0.66 us

profile of v5, /device:TPU:0, one launch (start us, length us, event | category | flops | bytes accessed | tf_op | source)
XLA Modules:
  0.0 12.9 jit_solution(14804479890563461342)
XLA Ops:
  0.6 11.6 %peridynamics.1 = (f32[2,8,512]{2,1,0:T(8,128)S(1)}, f32[2,8,512]{2,1,0:T(8,128)S(1)}, f32[8,512]{1,0:T(8,128)S(1)}) custom-call(f32[2,8,512]{2,1,0:T(8,128)} %disp.1, f32[2,8,512]{2,1,0:T(8,128)} %vel.1, f32[8,512]{1,0:T(8,128)} %pres.1, s32[10,8,512]{2,1,0:T(8,128)} %bits.1, s32[8,512]{1,0:T(8,128)} %klass.1, f32[4,4]{1,0:T(4,128)} %table.1), custom_call_target="tpu_custom_call" | custom-call | tf_op jit(solution)/shard_map/peridynamics/pallas_call | solution.py:644
  12.2 0.7 %hand_over.1 = (f32[2,8,512]{2,1,0:T(8,128)}, f32[2,8,512]{2,1,0:T(8,128)}, f32[8,512]{1,0:T(8,128)}) custom-call(f32[2,8,512]{2,1,0:T(8,128)S(1)} %get-tuple-element.6.a, f32[2,8,512]{2,1,0:T(8,128)S(1)} %get-tuple-element.7.b, f32[8,512]{1,0:T(8,128)S(1)} %get-tuple-element.8.c), custom_call_target="tpu_custom_call" | custom-call | tf_op jit(solution)/shard_map/hand_over/pallas_call | solution.py:693

commit v6 on v5

--- a/solution.py
+++ b/solution.py
@@ -87,6 +87,23 @@
     has_up, has_down = gx > 0, gx < gx_count - 1
     up, down, mate = gx - 1, gx + 1, 1 - gy
 
+    barrier = pltpu.get_barrier_semaphore()
+
+    def greet(x, y):
+        pl.semaphore_signal(barrier, inc=1, device_id=(sample, x, y), device_id_type=MESH)
+
+    @pl.when(has_up)
+    def _():
+        greet(up, gy)
+        greet(up, mate)
+
+    @pl.when(has_down)
+    def _():
+        greet(down, gy)
+        greet(down, mate)
+
+    greet(gx, mate)
+
     local = [
         pltpu.make_async_copy(table, table_s, local_sem.at[0]),
         pltpu.make_async_copy(klass, klass_v, local_sem.at[1]),
@@ -98,29 +115,25 @@
     for copy in local:
         copy.start()
 
-    for plane in range(4):
-        fill = float(OUTSIDE) if plane == 3 else 0.0
-        far1[plane] = jnp.full(far1.shape[1:], fill, f32)
-        if plane < 3:
-            far2[plane] = jnp.zeros(far2.shape[1:], f32)
-    far_pack[...] = jnp.full(far_pack.shape, float(OUTSIDE), f32)
-
-    barrier = pltpu.get_barrier_semaphore()
-
-    def greet(x, y):
-        pl.semaphore_signal(barrier, inc=1, device_id=(sample, x, y), device_id_type=MESH)
-
-    @pl.when(has_up)
+    def clear(rows):
+        count = rows.stop - rows.start
+        for ref, planes in ((far1, 4), (far2, 3)):
+            for plane in range(planes):
+                fill = float(OUTSIDE) if plane == 3 else 0.0
+                ref[plane, :blocks, rows, :] = jnp.full((blocks, count, LANES), fill, f32)
+        far_pack[:, rows, :] = jnp.full((2, count, LANES), float(OUTSIDE), f32)
+
+    clear(slice(0, ROWS - REACH))
+    clear(slice(ROWS + REACH, 2 * ROWS))
+
+    @pl.when(jnp.logical_not(has_up))
     def _():
-        greet(up, gy)
-        greet(up, mate)
-
-    @pl.when(has_down)
+        clear(slice(ROWS - REACH, ROWS))
+
+    @pl.when(jnp.logical_not(has_down))
     def _():
-        greet(down, gy)
-        greet(down, mate)
-
-    greet(gx, mate)
+        clear(slice(ROWS, ROWS + REACH))
+
 
     def cut(value):
         return [value[:, j * LANES : (j + 1) * LANES] for j in PLACES]

time: 13 us -> 13 us (level)
  no operation moved by 1% of the time
where the time goes in v6:
time: 13 us; the launch traced here: 12.9 us
  Pallas kernels  12.2 us (94%)
  between operations  0.64 us (5%)
    pallas_call x1, Pallas kernels, body(): pl.pallas_call(functools.partial(kernel, gx_count), out_shape=tuple((pltp...  11.6 us
    pallas_call x1, Pallas kernels, body(): pl.pallas_call(hand_over, out_shape=tuple((jax.ShapeDtypeStruct(s, f) for...  0.66 us

profile of v6, /device:TPU:0, one launch (start us, length us, event | category | flops | bytes accessed | tf_op | source)
XLA Modules:
  0.0 12.9 jit_solution(16364169351410859765)
XLA Ops:
  0.6 11.6 %peridynamics.1 = (f32[2,8,512]{2,1,0:T(8,128)S(1)}, f32[2,8,512]{2,1,0:T(8,128)S(1)}, f32[8,512]{1,0:T(8,128)S(1)}) custom-call(f32[2,8,512]{2,1,0:T(8,128)} %disp.1, f32[2,8,512]{2,1,0:T(8,128)} %vel.1, f32[8,512]{1,0:T(8,128)} %pres.1, s32[10,8,512]{2,1,0:T(8,128)} %bits.1, s32[8,512]{1,0:T(8,128)} %klass.1, f32[4,4]{1,0:T(4,128)} %table.1), custom_call_target="tpu_custom_call" | custom-call | tf_op jit(solution)/shard_map/peridynamics/pallas_call | solution.py:657
  12.2 0.7 %hand_over.1 = (f32[2,8,512]{2,1,0:T(8,128)}, f32[2,8,512]{2,1,0:T(8,128)}, f32[8,512]{1,0:T(8,128)}) custom-call(f32[2,8,512]{2,1,0:T(8,128)S(1)} %get-tuple-element.6.a, f32[2,8,512]{2,1,0:T(8,128)S(1)} %get-tuple-element.7.b, f32[8,512]{1,0:T(8,128)S(1)} %get-tuple-element.8.c), custom_call_target="tpu_custom_call" | custom-call | tf_op jit(solution)/shard_map/hand_over/pallas_call | solution.py:706

commit v7 on v6

--- a/solution.py
+++ b/solution.py
@@ -18,7 +18,7 @@
 RIM = len(PLACES)
 AFTER, BEFORE = (2, RIM, 3, 1), (RIM, 3, 0, 2)
 OUTER, INNER, ALL = (0, 1), (2, 3), (0, 1, 2, 3)
-MESSAGES = 14
+MESSAGES = 12
 STRIP = 16
 HALF = 4
 JOINED = (2, 3)

time: 13 us -> 13 us (level)
  no operation moved by 1% of the time
where the time goes in v7:
time: 13 us; the launch traced here: 12.8 us
  Pallas kernels  12.2 us (94%)
  between operations  0.64 us (5%)
    pallas_call x1, Pallas kernels, body(): pl.pallas_call(functools.partial(kernel, gx_count), out_shape=tuple((pltp...  11.5 us
    pallas_call x1, Pallas kernels, body(): pl.pallas_call(hand_over, out_shape=tuple((jax.ShapeDtypeStruct(s, f) for...  0.66 us

profile of v7, /device:TPU:0, one launch (start us, length us, event | category | flops | bytes accessed | tf_op | source)
XLA Modules:
  0.0 12.8 jit_solution(8689029575411892501)
XLA Ops:
  0.6 11.5 %peridynamics.1 = (f32[2,8,512]{2,1,0:T(8,128)S(1)}, f32[2,8,512]{2,1,0:T(8,128)S(1)}, f32[8,512]{1,0:T(8,128)S(1)}) custom-call(f32[2,8,512]{2,1,0:T(8,128)} %disp.1, f32[2,8,512]{2,1,0:T(8,128)} %vel.1, f32[8,512]{1,0:T(8,128)} %pres.1, s32[10,8,512]{2,1,0:T(8,128)} %bits.1, s32[8,512]{1,0:T(8,128)} %klass.1, f32[4,4]{1,0:T(4,128)} %table.1), custom_call_target="tpu_custom_call" | custom-call | tf_op jit(solution)/shard_map/peridynamics/pallas_call | solution.py:657
  12.2 0.7 %hand_over.1 = (f32[2,8,512]{2,1,0:T(8,128)}, f32[2,8,512]{2,1,0:T(8,128)}, f32[8,512]{1,0:T(8,128)}) custom-call(f32[2,8,512]{2,1,0:T(8,128)S(1)} %get-tuple-element.6.a, f32[2,8,512]{2,1,0:T(8,128)S(1)} %get-tuple-element.7.b, f32[8,512]{1,0:T(8,128)S(1)} %get-tuple-element.8.c), custom_call_target="tpu_custom_call" | custom-call | tf_op jit(solution)/shard_map/hand_over/pallas_call | solution.py:706
